TPU v7x, 512 devices: a whole 4x4x16 slice. The times are simulated.
512 devices in a mesh: ax: 16 (over y_hi, x, core), xs: 32 (over y_lo, z).
Axes of the slice: x: 4, y: 4 (y_hi: 2, y_lo: 2; y = y_hi * 2 + y_lo), z: 16, core: 2. Of those that a mesh axis runs over, the one named last changes fastest.
Arguments:
- concentrations_before: float32 [9, 192, 128, 1024], P(None, 'ax', 'xs'), may hold values from 0.05 to 1
- thermal_field_before: float32 [192, 128, 1024], P('ax', 'xs'), may hold values from 0.8 to 2.5
- flow_speed_vector: float32 [3, 192, 128, 1024], P(None, 'ax', 'xs'), may hold values from -4 to 4
- gap_indicator: int32 [192, 128, 1024], P('ax', 'xs'), may hold values 0 or 1
- destination_slice: int32 [192], replicated, may hold values from 0 to 191, as said below
- reaction_rate_constant: float32 [9], replicated, may hold values from 0.5 to 4
- threshold_kelvin: float32 [9], replicated, may hold values from 0.5 to 3
- reaction_coefficient_matrix: float32 [9, 9], replicated, may hold values from -2 to 2
- energy_release: float32 [9], replicated, may hold values from -4 to 4
- viewer_picture: float32 [128, 1024], P('xs', 'ax'), may hold values from 0 to 1.5
Outputs:
- concentrations_after: float32 [9, 192, 128, 1024], P(None, 'ax', 'xs')
- thermal_field_after: float32 [192, 128, 1024], P('ax', 'xs')
- image_error: float32 [128, 1024], P('xs', 'ax')
Inputs may be any that keep to these rules, and one draw needn't show every extreme that they name: destination_slice[p] = p minus the number of 2 distinct merge positions (each in 1 to 191) at or before p, one of which lies in 1 to 12; so destination_slice is nondecreasing, lies in [p - 2, p], and each new plane from 0 to 189 receives between one and 3 old planes (more than two only where merge positions are adjacent).
All inputs are finite; a program needn't handle non-finite values. No bound on the sum of `gap_indicator` on one device may be relied on, other than what follows from the above.
Results may differ from a plain program's by a relative error of at most 0.000053.
Values sent between devices are 32-bit elements; how exact they have to be, the bound alone decides.
A program may use at most 64 MiB of HBM per device.

v0:
```python
import jax
import jax.numpy as jnp
from jax import lax
from jax.sharding import PartitionSpec as P

SPECIES_TOTAL = 9
SHIFT = 2


def shifted(block, axis, distance):
    devices = range(lax.axis_size(axis))
    route = [(i - distance, i) for i in devices if i - distance in devices]
    return lax.ppermute(block, axis, route)


def with_halo(block, sides, width):
    for axis, dim in sides:
        count = lax.axis_size(axis)
        forward = [(i, i + 1) for i in range(count - 1)]
        backward = [(target, source) for source, target in forward]
        low = lax.ppermute(
            lax.slice_in_dim(block, block.shape[dim] - width, None, axis=dim), axis, forward
        )
        high = lax.ppermute(lax.slice_in_dim(block, 0, width, axis=dim), axis, backward)
        block = jnp.concatenate([low, block, high], axis=dim)
    return block


def split_up(x, dim, count):
    dims = x.shape
    parts = x.reshape(*dims[:dim], count, dims[dim] // count, *dims[dim + 1 :])
    return jnp.moveaxis(parts, dim, 0)


def sum_at_owner(x, axis, dim):
    count = lax.axis_size(axis)
    parts = lax.all_to_all(split_up(x, dim, count), axis, 0, 0, tiled=True)
    return jnp.sum(parts, axis=0)


def remap_planes(extended, owner_padded, first, count_new, fallback):
    owner_part = lax.dynamic_slice_in_dim(owner_padded, first + 1, extended.shape[1], 0)
    targets = first + jnp.arange(count_new, dtype=jnp.int32)
    onehot = (owner_part[None, :] == targets[:, None]).astype(jnp.float32)
    summed = jnp.einsum("qp,cpyz->cqyz", onehot, extended, precision=lax.Precision.HIGHEST)
    counts = jnp.sum(onehot, axis=1)
    scaled = summed / jnp.maximum(counts, 1.0)[None, :, None, None]
    return jnp.where((counts > 0.0)[None, :, None, None], scaled, fallback)


def chemistry(
    center, reaction_rate_constant, threshold_kelvin, reaction_coefficient_matrix, energy_release
):
    ys = center[:SPECIES_TOTAL]
    temp = center[SPECIES_TOTAL]
    rates = (
        reaction_rate_constant[:, None, None, None]
        * jnp.exp(-threshold_kelvin[:, None, None, None] / temp[None])
        * ys
        * jnp.roll(ys, -1, axis=0)
    )
    flat = rates.reshape(SPECIES_TOTAL, rates.shape[1], -1)
    source = jnp.einsum(
        "sr,ryz->syz", reaction_coefficient_matrix, flat, precision=lax.Precision.HIGHEST
    ).reshape(rates.shape)
    warming_source = jnp.einsum(
        "r,ryz->yz", energy_release, flat, precision=lax.Precision.HIGHEST
    ).reshape(rates.shape[1:])
    return (source, warming_source)


def per_device(
    concentrations_before,
    thermal_field_before,
    flow_speed_vector,
    gap_indicator,
    destination_slice,
    reaction_rate_constant,
    threshold_kelvin,
    reaction_coefficient_matrix,
    energy_release,
    viewer_picture,
):
    earlier_fields = jnp.concatenate([concentrations_before, thermal_field_before[None]], axis=0)
    planes = earlier_fields.shape[1]
    start = lax.axis_index("ax") * planes
    sentinel = jnp.full((SHIFT + 2,), -2, jnp.int32)
    owner_padded = jnp.concatenate([sentinel[:1], destination_slice, sentinel], axis=0)
    upper = shifted(earlier_fields[:, : SHIFT + 1], "ax", -1)
    extended = jnp.concatenate([earlier_fields, upper], axis=1)
    above = remap_planes(extended, owner_padded, start, planes + 1, extended[:, : planes + 1])
    remapped = above[:, :planes]
    lower = shifted(remapped[:, planes - 1 :], "ax", 1)
    axial_pad = jnp.concatenate([lower, above], axis=1)
    side_pad = with_halo(remapped, (("xs", 2),), 1)
    upper_a = axial_pad[:, 2:]
    lower_a = axial_pad[:, :-2]
    upper_y = side_pad[:, :, 2:]
    lower_y = side_pad[:, :, :-2]
    zero_column = jnp.zeros(remapped.shape[:3] + (1,), jnp.float32)
    upper_z = jnp.concatenate([remapped[..., 1:], zero_column], axis=3)
    lower_z = jnp.concatenate([zero_column, remapped[..., :-1]], axis=3)
    lap = upper_a + lower_a + upper_y + lower_y + upper_z + lower_z - 6.0 * remapped
    adv = 0.5 * (
        flow_speed_vector[0][None] * (upper_a - lower_a)
        + flow_speed_vector[1][None] * (upper_y - lower_y)
        + flow_speed_vector[2][None] * (upper_z - lower_z)
    )
    advective_current = remapped + 0.1 * lap - 0.2 * adv
    source, warming_source = chemistry(
        remapped,
        reaction_rate_constant,
        threshold_kelvin,
        reaction_coefficient_matrix,
        energy_release,
    )
    fluid_blend = (1 - gap_indicator).astype(jnp.float32)
    concentrations_after = advective_current[:SPECIES_TOTAL] + 0.5 * fluid_blend[None] * source
    thermal_field_after = advective_current[SPECIES_TOTAL] + 0.5 * fluid_blend * warming_source
    whole_slice_group = planes * lax.axis_size("ax")
    local_frame_part = (
        jnp.sum(fluid_blend * concentrations_after[4] * thermal_field_after, axis=0)
        / whole_slice_group
    )
    glow_picture = sum_at_owner(local_frame_part, "ax", 1)
    return (concentrations_after, thermal_field_after, glow_picture - viewer_picture)


def solution(mesh):
    in_specs = (
        P(None, "ax", "xs", None),
        P("ax", "xs", None),
        P(None, "ax", "xs", None),
        P("ax", "xs", None),
        P(),
        P(),
        P(),
        P(),
        P(),
        P("xs", "ax"),
    )
    out_specs = (P(None, "ax", "xs", None), P("ax", "xs", None), P("xs", "ax"))
    return jax.shard_map(
        per_device, mesh=mesh, in_specs=in_specs, out_specs=out_specs, check_vma=False
    )
```

profile of v0, /device:TPU:9, one launch (start us, length us, event | category | flops | bytes accessed | tf_op | source)
XLA Modules:
  0.0 95.1 jit_solution(2559231234842835297)
XLA Ops:
  0.6 0.0 copy-start
  0.6 1.0 %copy.96 = f32[12,4,1024]{2,0,1:T(8,128)S(1)} copy(f32[12,4,1024]{2,1,0:T(4,128)} %param.11) | data formatting | bytes 393216 | tf_op args[1]
  1.7 2.6 %copy.52 = f32[9,12,4,1024]{3,1,2,0:T(8,128)S(1)} copy(f32[9,12,4,1024]{3,2,1,0:T(4,128)} %param.10) | data formatting | bytes 3538944 | tf_op args[0]
  4.3 0.0 copy-start.7
  4.3 0.1 pad_maximum_fusion.4
  4.4 0.0 copy-start.10
  4.4 1.1 %copy.53 = f32[10,3,4,1024]{3,2,1,0:T(4,128)} copy(f32[10,3,4,1024]{3,1,2,0:T(4,128)S(1)} %pad_maximum_fusion.4) | data formatting | bytes 983040 | tf_op jit(solution)/shard_map/slice | solution.py:89
  5.5 2.6 %collective-permute-start = (f32[10,3,4,1024]{3,2,1,0:T(4,128)}, f32[10,3,4,1024]{3,2,1,0:T(4,128)}, u32[]{:S(2)}, u32[]{:S(2)}) collective-permute-start(f32[10,3,4,1024]{3,2,1,0:T(4,128)} %copy.53), channel_id=1, source_target_pairs={{32,0},{64,32},{96,64},{128,96},{160,128},{192,160},{224,192},{256... | collective-permute-start | bytes 1474568 | tf_op jit(solution)/shard_map/ppermute | solution.py:13
  8.1 1.8 %slice_bitcast_fusion.5 = (f32[12,4,1024]{2,1,0:T(4,128)}, f32[12,4,1024]{2,1,0:T(4,128)S(1)}, f32[12,4,1024]{2,1,0:T(4,128)S(1)}) fusion(f32[3,12,4,1024]{3,2,1,0:T(4,128)} %param.12), kind=kLoop, calls=%fused_computation.31 | loop fusion | bytes 1179648 | tf_op jit(solution)/shard_map/mul | solution.py:105
  9.9 0.0 copy-done.7
  9.9 0.1 pad_add_fusion
  10.0 0.1 dynamic_slice.3
  10.1 0.2 fusion.12
  10.3 0.1 copy.61
  10.4 0.1 copy.60
  10.5 1.0 %copy.59 = f32[12,4,1024]{2,0,1:T(8,128)S(1)} copy(f32[12,4,1024]{2,1,0:T(4,128)} %get-tuple-element.23) | data formatting | bytes 393216 | tf_op jit(solution)/shard_map/mul | solution.py:105
  11.6 0.0 copy-done.10
  11.6 1.8 %fusion.11 = f32[12,4,1024]{2,0,1:T(8,128)} fusion(s32[12,4,1024]{2,1,0:T(4,128)} %param.13), kind=kLoop, calls=%fused_computation.27 | loop fusion | flops 147456 | bytes 393216 | tf_op jit(solution)/shard_map/mul | solution.py:118
  13.4 2.6 %collective-permute-done = f32[10,3,4,1024]{3,2,1,0:T(4,128)} collective-permute-done((f32[10,3,4,1024]{3,2,1,0:T(4,128)}, f32[10,3,4,1024]{3,2,1,0:T(4,128)}, u32[]{:S(2)}, u32[]{:S(2)}) %collective-permute-start) | collective-permute-done | bytes 491552 | tf_op jit(solution)/shard_map/ppermute | solution.py:13
  16.0 1.4 %copy.54 = f32[10,3,4,1024]{3,1,2,0:T(4,128)S(1)} copy(f32[10,3,4,1024]{3,2,1,0:T(4,128)} %collective-permute-done) | data formatting | bytes 983040 | tf_op jit(solution)/shard_map/ppermute | solution.py:13
  17.4 0.4 pad_maximum_fusion.3
  17.7 2.0 %slice_select_fusion = f32[10,13,4,1024]{3,1,2,0:T(8,128)S(1)} fusion(f32[10,15,4,1024]{3,1,2,0:T(8,128)S(1)} %pad_maximum_fusion.3, f32[13]{0:T(128)S(1)} %broadcast_maximum_fusion, pred[13]{0:T(512)(128)(4,1)S(1)} %broadcast_compare_fusion, s32[15]{0:T(128)S(1)} %dynamic_slice.3, s32[13]{0:T(128)S(1)} %iota_add_fusion), kind=kOutput, calls=%fused_computation.7 | convolution fusion | flops 96911552 | bytes 7374848 | tf_op jit(solution)/shard_map/qp,cpyz->cqyz/dot_general | solution.py:45
  19.7 3.2 %fusion.19 = (f32[10,12,4,1023]{3,1,2,0:T(8,128)}, f32[10,12,4,1023]{3,1,2,0:T(8,128)}) fusion(f32[10,13,4,1024]{3,1,2,0:T(8,128)S(1)} %slice_select_fusion), kind=kLoop, calls=%fused_computation.45 | loop fusion | bytes 7856640 | tf_op jit(solution)/shard_map/slice | solution.py:101
  22.9 0.1 fusion.18
  23.1 0.8 slice.104
  23.9 0.0 copy-start.8
  24.0 0.1 slice.112
  24.1 1.3 %copy.57 = f32[10,12,1,1024]{3,2,1,0:T(1,128)} copy(f32[10,12,1,1024]{3,1,2,0:T(8,128)S(1)} %get-tuple-element.20) | data formatting | bytes 983040 | tf_op jit(solution)/shard_map/slice | solution.py:22
  25.4 3.5 %collective-permute-start.3 = (f32[10,12,1,1024]{3,2,1,0:T(1,128)}, f32[10,12,1,1024]{3,2,1,0:T(1,128)}, u32[]{:S(2)}, u32[]{:S(2)}) collective-permute-start(f32[10,12,1,1024]{3,2,1,0:T(1,128)} %copy.57), channel_id=1, source_target_pairs={{0,1},{1,2},{2,3},{3,4},{4,5},{5,6},{6,7},{7,8},{8,9},{9,10},{10,1... | collective-permute-start | bytes 1474568 | tf_op jit(solution)/shard_map/ppermute | solution.py:21
  28.9 1.3 %copy.55 = f32[10,12,1,1024]{3,2,1,0:T(1,128)} copy(f32[10,12,1,1024]{3,1,2,0:T(8,128)S(1)} %get-tuple-element.19) | data formatting | bytes 983040 | tf_op jit(solution)/shard_map/slice | solution.py:24
  30.2 9.4 %collective-permute-start.2 = (f32[10,12,1,1024]{3,2,1,0:T(1,128)}, f32[10,12,1,1024]{3,2,1,0:T(1,128)}, u32[]{:S(2)}, u32[]{:S(2)}) collective-permute-start(f32[10,12,1,1024]{3,2,1,0:T(1,128)} %copy.55), channel_id=1, source_target_pairs={{1,0},{2,1},{3,2},{4,3},{5,4},{6,5},{7,6},{8,7},{9,8},{10,9},{11,1... | collective-permute-start | bytes 1474568 | tf_op jit(solution)/shard_map/ppermute | solution.py:24
  39.6 2.0 %collective-permute-start.1 = (f32[10,1,4,1024]{3,1,2,0:T(1,128)}, f32[10,1,4,1024]{3,1,2,0:T(1,128)}, u32[]{:S(2)}, u32[]{:S(2)}) collective-permute-start(f32[10,1,4,1024]{3,1,2,0:T(1,128)} %slice.104), channel_id=1, source_target_pairs={{0,32},{32,64},{64,96},{96,128},{128,160},{160,192},{192,224},{224... | collective-permute-start | bytes 491528 | tf_op jit(solution)/shard_map/ppermute | solution.py:13
  41.7 0.0 copy-done.8
  41.7 0.7 fusion.5
  42.4 2.4 %copy.63 = f32[9,12,4,1024]{3,2,1,0:T(4,128)} copy(f32[9,12,4,1024]{3,1,2,0:T(8,128)S(1)} %fusion.5) | data formatting | bytes 3538944 | tf_op jit(solution)/shard_map/mul | solution.py:57
  44.8 3.5 %reshape.34 = f32[9,12,4096]{2,1,0:T(8,128)} reshape(f32[9,12,4,1024]{3,2,1,0:T(4,128)} %copy.63) | data formatting | bytes 3538944 | tf_op jit(solution)/shard_map/reshape | solution.py:62
  48.2 7.7 %convolution_bitcast_fusion = f32[9,12,4096]{2,0,1:T(8,128)} fusion(f32[9,12,4096]{2,1,0:T(8,128)} %reshape.34, f32[9,9]{1,0:T(8,128)S(1)} %copy-done), kind=kOutput, calls=%fused_computation | convolution fusion | flops 47775744 | bytes 3539268 | tf_op jit(solution)/shard_map/sr,ryz->syz/dot_general | solution.py:63
  55.9 3.5 %reshape.40 = f32[9,12,4,1024]{3,2,0,1:T(4,128)} reshape(f32[9,12,4096]{2,0,1:T(8,128)} %convolution_bitcast_fusion) | data formatting | bytes 3538944 | tf_op jit(solution)/shard_map/reshape | solution.py:65
  59.4 3.5 %dot_general.19 = f32[12,4,1024,9]{2,1,0,3:T(4,128)} reshape(f32[12,4096,9]{1,0,2:T(8,128)} %bitcast.55) | data formatting | bytes 3538944 | tf_op jit(solution)/shard_map/r,ryz->yz/dot_general | solution.py:66
  62.9 0.0 copy-done.9
  62.9 5.8 %fusion = f32[1,12,4,1024]{3,0,2,1:T(1,128)S(1)} fusion(f32[12,4,1024,9]{2,1,0,3:T(4,128)} %dot_general.19, f32[9]{0:T(128)S(1)} %copy-done.9), kind=kOutput, calls=%fused_computation.1 | convolution fusion | flops 5308416 | bytes 1966116 | tf_op jit(solution)/shard_map/r,ryz->yz/dot_general | solution.py:66
  68.7 0.0 collective-permute-done.3
  68.7 1.1 %copy.58 = f32[10,12,1,1024]{3,1,2,0:T(8,128)S(1)} copy(f32[10,12,1,1024]{3,2,1,0:T(1,128)} %collective-permute-done.3) | data formatting | bytes 983040 | tf_op jit(solution)/shard_map/ppermute | solution.py:21
  69.8 0.0 collective-permute-done.2
  69.9 1.1 %copy.56 = f32[10,12,1,1024]{3,1,2,0:T(8,128)S(1)} copy(f32[10,12,1,1024]{3,2,1,0:T(1,128)} %collective-permute-done.2) | data formatting | bytes 983040 | tf_op jit(solution)/shard_map/ppermute | solution.py:24
  71.0 0.0 collective-permute-done.1
  71.0 0.0 copy-done.1
  71.0 0.0 copy-done.2
  71.0 0.0 copy-start.3
  71.0 4.3 %multiply_subtract_fusion = f32[10,12,4,1024]{3,1,2,0:T(8,128)S(1)} fusion(f32[10,12,4,1024]{3,1,2,0:T(8,128)S(1)} %bitcast.54, f32[10,12,4,1023]{3,1,2,0:T(8,128)S(1)} %copy-done.2, f32[10,12,4,1023]{3,1,2,0:T(8,128)S(1)} %copy-done.1, f32[10,12,1,1024]{3,1,2,0:T(8,128)S(1)} %copy.58, f32[10,12,1,1024]{3,1,2,0:T(8,128)S(1)} %copy.56, ...), kind=kLoop, calls=%fused_computation.9 | loop fusion | flops 10813440 | bytes 17334272 | tf_op jit(solution)/shard_map/sub | solution.py:109
  75.4 0.0 copy-start.5
  75.4 1.3 %slice_add_fusion = f32[9,12,4,1024]{3,1,2,0:T(8,128)S(1)} fusion(f32[10,12,4,1024]{3,1,2,0:T(8,128)S(1)} %multiply_subtract_fusion, f32[9,12,4,1024]{3,2,0,1:T(4,128)S(1)} %copy-done.3, f32[12,4,1024]{2,0,1:T(8,128)S(1)} %copy-done.4), kind=kLoop, calls=%fused_computation.14 | loop fusion | flops 884736 | bytes 5505024 | tf_op jit(solution)/shard_map/add | solution.py:118
  76.7 0.3 fusion.8
  77.0 0.0 copy-start.6
  77.0 0.1 div.43
  77.1 0.7 reshape.41
  77.8 8.0 %all-to-all-start = ((f32[16,1,256]{2,1,0:T(1,128)}), f32[16,1,256]{2,1,0:T(1,128)S(1)}, u32[]{:S(2)}, u32[]{:S(2)}) async-start(f32[16,1,256]{2,1,0:T(1,128)} %reshape.41), calls=%async_computation | async-start | bytes 32768 | tf_op jit(solution)/shard_map/all_to_all | solution.py:37
  85.9 2.4 %copy.68 = f32[9,12,4,1024]{3,2,1,0:T(4,128)} copy(f32[9,12,4,1024]{3,1,2,0:T(8,128)S(1)} %slice_add_fusion) | data formatting | bytes 3538944
  88.2 0.8 copy.69
  89.0 4.1 %all-to-all-done = f32[16,1,256]{2,1,0:T(1,128)S(1)} async-done(((f32[16,1,256]{2,1,0:T(1,128)}), f32[16,1,256]{2,1,0:T(1,128)S(1)}, u32[]{:S(2)}, u32[]{:S(2)}) %all-to-all-start) | async-done | bytes 16416 | tf_op jit(solution)/shard_map/all_to_all | solution.py:37
  93.1 0.5 broadcast.41
  93.7 0.7 reduce
  94.4 0.1 reshape.42
  94.5 0.6 sub.31
  (18 shorter events, 0.1 us)
Async XLA Ops:
  0.6 47.6 %copy-start = (f32[9,9]{1,0:T(8,128)S(1)}, f32[9,9]{1,0:T(8,128)}, u32[]{:S(2)}) copy-start(f32[9,9]{1,0:T(8,128)} %param.17) | copy-start | bytes 976
  4.3 5.7 %copy-start.7 = (s32[192]{0:T(256)S(1)}, s32[192]{0:T(256)}, u32[]{:S(2)}) copy-start(s32[192]{0:T(256)} %param.14) | copy-start | bytes 2308
  4.4 7.2 %copy-start.10 = (f32[9]{0:T(128)S(1)}, f32[9]{0:T(128)}, u32[]{:S(2)}) copy-start(f32[9]{0:T(128)} %param.16) | copy-start | bytes 112
  5.5 10.5 %collective-permute-start = (f32[10,3,4,1024]{3,2,1,0:T(4,128)}, f32[10,3,4,1024]{3,2,1,0:T(4,128)}, u32[]{:S(2)}, u32[]{:S(2)}) collective-permute-start(f32[10,3,4,1024]{3,2,1,0:T(4,128)} %copy.53), channel_id=1, source_target_pairs={{32,0},{64,32},{96,64},{128,96},{160,128},{192,160},{224,192},{256... | collective-permute-start | bytes 1474568 | tf_op jit(solution)/shard_map/ppermute | solution.py:13
  23.9 17.7 %copy-start.8 = (f32[9]{0:T(128)S(1)}, f32[9]{0:T(128)}, u32[]{:S(2)}) copy-start(f32[9]{0:T(128)} %param.15) | copy-start | bytes 112
  25.4 43.3 %collective-permute-start.3 = (f32[10,12,1,1024]{3,2,1,0:T(1,128)}, f32[10,12,1,1024]{3,2,1,0:T(1,128)}, u32[]{:S(2)}, u32[]{:S(2)}) collective-permute-start(f32[10,12,1,1024]{3,2,1,0:T(1,128)} %copy.57), channel_id=1, source_target_pairs={{0,1},{1,2},{2,3},{3,4},{4,5},{5,6},{6,7},{7,8},{8,9},{9,10},{10,1... | collective-permute-start | bytes 1474568 | tf_op jit(solution)/shard_map/ppermute | solution.py:21
  30.2 39.6 %collective-permute-start.2 = (f32[10,12,1,1024]{3,2,1,0:T(1,128)}, f32[10,12,1,1024]{3,2,1,0:T(1,128)}, u32[]{:S(2)}, u32[]{:S(2)}) collective-permute-start(f32[10,12,1,1024]{3,2,1,0:T(1,128)} %copy.55), channel_id=1, source_target_pairs={{1,0},{2,1},{3,2},{4,3},{5,4},{6,5},{7,6},{8,7},{9,8},{10,9},{11,1... | collective-permute-start | bytes 1474568 | tf_op jit(solution)/shard_map/ppermute | solution.py:24
  39.6 31.4 %collective-permute-start.1 = (f32[10,1,4,1024]{3,1,2,0:T(1,128)}, f32[10,1,4,1024]{3,1,2,0:T(1,128)}, u32[]{:S(2)}, u32[]{:S(2)}) collective-permute-start(f32[10,1,4,1024]{3,1,2,0:T(1,128)} %slice.104), channel_id=1, source_target_pairs={{0,32},{32,64},{64,96},{96,128},{128,160},{160,192},{192,224},{224... | collective-permute-start | bytes 491528 | tf_op jit(solution)/shard_map/ppermute | solution.py:13
  59.4 3.5 %copy-start.9 = (f32[9]{0:T(128)S(1)}, f32[9]{0:T(128)}, u32[]{:S(2)}) copy-start(f32[9]{0:T(128)} %param.18) | copy-start | bytes 112
  62.9 8.1 %copy-start.1 = (f32[10,12,4,1023]{3,1,2,0:T(8,128)S(1)}, f32[10,12,4,1023]{3,1,2,0:T(8,128)}, u32[]{:S(2)}) copy-start(f32[10,12,4,1023]{3,1,2,0:T(8,128)} %get-tuple-element.21) | copy-start | bytes 5892484
  62.9 8.1 %copy-start.2 = (f32[10,12,4,1023]{3,1,2,0:T(8,128)S(1)}, f32[10,12,4,1023]{3,1,2,0:T(8,128)}, u32[]{:S(2)}) copy-start(f32[10,12,4,1023]{3,1,2,0:T(8,128)} %get-tuple-element.22) | copy-start | bytes 5892484
  71.0 4.3 %copy-start.3 = (f32[9,12,4,1024]{3,2,0,1:T(4,128)S(1)}, f32[9,12,4,1024]{3,2,0,1:T(4,128)}, u32[]{:S(2)}) copy-start(f32[9,12,4,1024]{3,2,0,1:T(4,128)} %reshape.40) | copy-start | bytes 5308420
  71.0 4.3 %copy-start.4 = (f32[12,4,1024]{2,0,1:T(8,128)S(1)}, f32[12,4,1024]{2,0,1:T(8,128)}, u32[]{:S(2)}) copy-start(f32[12,4,1024]{2,0,1:T(8,128)} %fusion.11) | copy-start | bytes 589828
  75.4 1.3 %copy-start.5 = (s32[12,4,1024]{2,1,0:T(4,128)S(1)}, s32[12,4,1024]{2,1,0:T(4,128)}, u32[]{:S(2)}) copy-start(s32[12,4,1024]{2,1,0:T(4,128)} %param.13) | copy-start | bytes 589828
  77.0 17.5 %copy-start.6 = (f32[4,64]{1,0:T(4,128)S(1)}, f32[4,64]{1,0:T(4,128)}, u32[]{:S(2)}) copy-start(f32[4,64]{1,0:T(4,128)} %param.19) | copy-start | bytes 3076
  77.8 15.3 %all-to-all-start = ((f32[16,1,256]{2,1,0:T(1,128)}), f32[16,1,256]{2,1,0:T(1,128)S(1)}, u32[]{:S(2)}, u32[]{:S(2)}) async-start(f32[16,1,256]{2,1,0:T(1,128)} %reshape.41), calls=%async_computation | async-start | bytes 32768 | tf_op jit(solution)/shard_map/all_to_all | solution.py:37
where the time goes:
time: 95.7 us; the launch traced here: 95.1 us
  local copies, waits for them, and re-layouts  35.9 us (38%)
  starting transfers between devices  25.5 us (27%)
  matrix products  15.4 us (16%)
  other arithmetic  10.5 us (11%)
  waiting for transfers between devices  6.73 us (7%)
  between operations  0.98 us (1%)
    ppermute x1, starting transfers between devices, with_halo(): lax.ppermute(lax.slice_in_dim(block, 0, width, axis=dim), axis, backward)  9.37 us
    all_to_all x1, starting transfers between devices, sum_at_owner(): parts = lax.all_to_all(split_up(x, dim, count), axis, 0, 0, tiled=True)  8.02 us
    dot_general x1, matrix products, chemistry(): jnp.einsum('sr,ryz->syz', reaction_coefficient_matrix, flat, precision=la...  7.67 us
    unnamed x28, local copies, waits for them, and re-layouts  7.61 us
    dot_general x1, matrix products, chemistry(): jnp.einsum('r,ryz->yz', energy_release, flat, precision=lax.Precision.HIG...  5.79 us
    ppermute x2, starting transfers between devices, shifted(): return lax.ppermute(block, axis, route)  4.6 us
    sub x1, other arithmetic, per_device(): advective_current = remapped + 0.1 * lap - 0.2 * adv  4.3 us
    all_to_all x1, waiting for transfers between devices, sum_at_owner(): parts = lax.all_to_all(split_up(x, dim, count), axis, 0, 0, tiled=True)  4.12 us
  transfers between devices with their start and end apart: 5, of which 2 were waited for; matrix products, arithmetic and copies ran while one was open for 41% of the time, Pallas kernels for 0%

commit v1 on v0

v1 whole, which is shorter than its diff:
```python
import functools

import jax
import jax.numpy as jnp
from jax import lax
from jax.experimental import pallas as pl
from jax.experimental.pallas import tpu as pltpu
from jax.sharding import PartitionSpec as P

SPECIES = 9
FIELDS = 10
ORDER = (9, 4, 0, 1, 2, 3, 5, 6, 7, 8)
PLACE = tuple(ORDER.index(f) for f in range(FIELDS))
GROUPS = ((0, 2), (2, 4), (6, 4))
ROWS = 4
LANES = 128
CHUNKS = 8
MESH = pl.DeviceIdType.MESH


def per_device_kernel(
    n_ax, n_xs, planes, total_planes,
    conc, temp, vel, gap, dest, rate_k, thresh, coeff, heat, picture,
    conc_out, temp_out, image_out,
    old, rem, vel_v, gap_v, coef, edge, gas, mix, img, img_in,
    load_sem, small_sem, ax_send, ax_recv, xs_send, xs_recv, img_send, img_recv,
    dest_s, rate_s, thresh_s, coeff_s, heat_s, picture_v,
):
    ax = lax.axis_index("ax")
    xs = lax.axis_index("xs")
    start = ax * planes

    barrier = pltpu.get_barrier_semaphore()
    for d in range(1, n_ax):
        pl.semaphore_signal(
            barrier, inc=1, device_id=(lax.rem(ax + d, n_ax), xs), device_id_type=MESH
        )
    for d in (1, n_xs - 1):
        pl.semaphore_signal(
            barrier, inc=1, device_id=(ax, lax.rem(xs + d, n_xs)), device_id_type=MESH
        )

    def local(src, dst, sem):
        copy = pltpu.make_async_copy(src, dst, sem)
        copy.start()
        return copy

    smalls = [
        local(dest, dest_s, small_sem.at[0]),
        local(rate_k, rate_s, small_sem.at[1]),
        local(thresh, thresh_s, small_sem.at[2]),
        local(coeff, coeff_s, small_sem.at[3]),
        local(heat, heat_s, small_sem.at[4]),
        local(picture, picture_v, small_sem.at[5]),
    ]
    own = pl.ds(1, planes)
    loads = [
        local(temp, old.at[0, own], load_sem.at[0]),
        local(conc.at[4], old.at[1, own], load_sem.at[1]),
        local(conc.at[pl.ds(0, 4)], old.at[pl.ds(2, 4), own], load_sem.at[2]),
        local(conc.at[pl.ds(5, 4)], old.at[pl.ds(6, 4), own], load_sem.at[3]),
        local(vel, vel_v, load_sem.at[4]),
        local(gap, gap_v, load_sem.at[5]),
    ]

    @pl.when(ax == 0)
    def _():
        old[:, 0] = jnp.zeros((FIELDS, 32, LANES), jnp.float32)

    @pl.when(ax == n_ax - 1)
    def _():
        old[:, pl.ds(planes + 1, 3)] = jnp.zeros((FIELDS, 3, 32, LANES), jnp.float32)

    img[...] = jnp.zeros_like(img)

    def row(r):
        return pl.ds(r, CHUNKS, stride=ROWS)

    def weights(q):
        new = start + q

        def hit(k):
            p = jnp.clip(new + k, 0, total_planes - 1)
            good = (dest_s[p] == new) & (new + k < total_planes) & (new + k >= 0)
            return good.astype(jnp.int32)

        h = [hit(k) for k in range(3)]
        count = h[0] + h[1] + h[2]
        inv = jnp.where(count == 3, 1.0 / 3.0, jnp.where(count == 2, 0.5, 1.0)).astype(
            jnp.float32
        )
        inside = ((new >= 0) & (new < total_planes)).astype(jnp.int32)
        none = (count == 0).astype(jnp.int32) * inside
        first = (h[0] + none).astype(jnp.float32) * inv
        return first, h[1].astype(jnp.float32) * inv, h[2].astype(jnp.float32) * inv

    def remap(first_field, fields, q0, count):
        def body(i, carry):
            q = q0 + i
            w = weights(q)
            for f in range(first_field, first_field + fields):
                for r in range(ROWS):
                    rem[f, q + 1, r + 1] = (
                        w[0] * old[f, q + 1, row(r), :]
                        + w[1] * old[f, q + 2, row(r), :]
                        + w[2] * old[f, q + 3, row(r), :]
                    )
            return carry

        lax.fori_loop(0, count, body, 0)

    def remap_low(first_field, fields):
        w = weights(-1)
        for f in range(first_field, first_field + fields):
            for r in range(ROWS):
                rem[f, 0, r + 1] = (
                    w[0] * old[f, 0, row(r), :]
                    + w[1] * old[f, 1, row(r), :]
                    + w[2] * old[f, 2, row(r), :]
                )

    down = (lax.max(ax - 1, 0), xs)
    up = (lax.min(ax + 1, n_ax - 1), xs)
    low3, top3 = pl.ds(0, 3), pl.ds(planes + 1, 3)
    ax_parts = (
        (lambda s: temp.at[s], (0,)),
        (lambda s: conc.at[4, s], (1,)),
        (lambda s: conc.at[pl.ds(0, 4), s], (pl.ds(2, 4),)),
        (lambda s: conc.at[pl.ds(5, 4), s], (pl.ds(6, 4),)),
    )

    def ax_copy(part, going_down):
        source, where = ax_parts[part]
        slot = 2 * part + (0 if going_down else 1)
        return pltpu.make_async_remote_copy(
            src_ref=source(low3 if going_down else planes - 1),
            dst_ref=old.at[where + ((top3 if going_down else 0),)],
            send_sem=ax_send.at[slot],
            recv_sem=ax_recv.at[slot],
            device_id=down if going_down else up,
            device_id_type=MESH,
        )

    spans = (pl.ds(1, planes - 2), pl.ds(planes - 1, 2))

    def xs_copy(group, span, going_down):
        f0, fn = GROUPS[group]
        slot = 4 * group + 2 * span + (0 if going_down else 1)
        fields = pl.ds(f0, fn)
        return pltpu.make_async_remote_copy(
            src_ref=rem.at[fields, spans[span], 1 if going_down else ROWS],
            dst_ref=rem.at[fields, spans[span], ROWS + 1 if going_down else 0],
            send_sem=xs_send.at[slot],
            recv_sem=xs_recv.at[slot],
            device_id=(ax, lax.max(xs - 1, 0) if going_down else lax.min(xs + 1, n_xs - 1)),
            device_id_type=MESH,
        )

    def xs_start(group, span):
        @pl.when(xs > 0)
        def _():
            xs_copy(group, span, True).start()

        @pl.when(xs < n_xs - 1)
        def _():
            xs_copy(group, span, False).start()

    smalls[0].wait()
    loads[0].wait()
    loads[1].wait()
    remap(0, 2, 0, planes - 2)
    pl.semaphore_wait(barrier, n_ax + 1)

    for part in range(4):
        @pl.when(ax > 0)
        def _():
            ax_copy(part, True).start()

        @pl.when(ax < n_ax - 1)
        def _():
            ax_copy(part, False).start()

    xs_start(0, 0)
    loads[2].wait()
    remap(2, 4, 0, planes - 2)
    xs_start(1, 0)
    loads[3].wait()
    remap(6, 4, 0, planes - 2)
    xs_start(2, 0)
    for small in smalls[1:]:
        small.wait()
    loads[4].wait()
    loads[5].wait()

    for s in range(SPECIES):
        for r in range(SPECIES):
            mix[s * SPECIES + r] = coeff_s[s, r] * rate_s[r]
    for r in range(SPECIES):
        mix[SPECIES * SPECIES + r] = heat_s[r] * rate_s[r]

    lane = lax.broadcasted_iota(jnp.int32, (CHUNKS, LANES), 1)
    chunk = lax.broadcasted_iota(jnp.int32, (CHUNKS, LANES), 0)
    at_last = lane == LANES - 1
    at_first = lane == 0
    z_end = at_last & (chunk == CHUNKS - 1)
    z_begin = at_first & (chunk == 0)

    def out_ref(i):
        f = ORDER[i]
        return temp_out if f == SPECIES else conc_out.at[f]

    def plane(q):
        for r in range(ROWS):
            for d in range(3):
                v = 0.1 * vel_v[d, q, row(r), :]
                above = 0.1 - v
                below = 0.1 + v
                if d == 2:
                    above = jnp.where(z_end, 0.0, above)
                    below = jnp.where(z_begin, 0.0, below)
                if d == 1 and r == 0:
                    edge[q, 0] = below
                if d == 1 and r == ROWS - 1:
                    edge[q, 1] = above
                coef[2 * d, r] = above
                coef[2 * d + 1, r] = below
            gas[q, r] = 0.5 * (1 - gap_v[q, row(r), :]).astype(jnp.float32)
        rates = []
        for r in range(ROWS):
            inv = -1.0 / rem[0, q + 1, r + 1]
            ys = [rem[PLACE[s], q + 1, r + 1] for s in range(SPECIES)]
            rates.append(
                [
                    jnp.exp(thresh_s[s] * inv) * (ys[s] * ys[(s + 1) % SPECIES])
                    for s in range(SPECIES)
                ]
            )
        for i in range(FIELDS):
            f = ORDER[i]
            source = [None] * ROWS
            for s in range(SPECIES):
                m = mix[f * SPECIES + s]
                for r in range(ROWS):
                    term = m * rates[r][s]
                    source[r] = term if source[r] is None else source[r] + term
            mine = [rem[i, q + 1, r + 1] for r in range(ROWS)]
            for r in range(ROWS):
                x = mine[r]
                to_up = pltpu.roll(x, LANES - 1, 1)
                to_up = jnp.where(at_last, pltpu.roll(to_up, CHUNKS - 1, 0), to_up)
                to_low = pltpu.roll(x, 1, 1)
                to_low = jnp.where(at_first, pltpu.roll(to_low, 1, 0), to_low)
                total = 0.4 * x + gas[q, r] * source[r]
                total += coef[0, r] * rem[i, q + 2, r + 1] + coef[1, r] * rem[i, q, r + 1]
                total += coef[4, r] * to_up + coef[5, r] * to_low
                if r > 0:
                    total += coef[3, r] * mine[r - 1]
                if r < ROWS - 1:
                    total += coef[2, r] * mine[r + 1]
                out_ref(i)[q, row(r), :] = total

    def run_planes(first, count):
        def body(i, carry):
            plane(first + i)
            return carry

        lax.fori_loop(0, count, body, 0)

    run_planes(1, planes - 4)

    for group, parts in enumerate(((0, 1), (2,), (3,))):
        for part in parts:
            @pl.when(ax < n_ax - 1)
            def _():
                ax_copy(part, True).wait_recv()

            @pl.when(ax > 0)
            def _():
                ax_copy(part, False).wait_recv()
        f0, fn = GROUPS[group]
        remap(f0, fn, planes - 2, 3)
        xs_start(group, 1)
        remap_low(f0, fn)

    run_planes(0, 1)
    run_planes(planes - 3, 3)

    def add_rows(group):
        f0, fn = GROUPS[group]

        def side(is_low):
            r = 0 if is_low else ROWS - 1
            halo = 0 if is_low else ROWS + 1

            def body(q, carry):
                c = edge[q, 0 if is_low else 1]
                for i in range(f0, f0 + fn):
                    ref = out_ref(i)
                    ref[q, row(r), :] = ref[q, row(r), :] + c * rem[i, q + 1, halo]
                return carry

            for span in range(2):
                xs_copy(group, span, not is_low).wait_recv()
            lax.fori_loop(0, planes, body, 0)

        @pl.when(xs > 0)
        def _():
            side(True)

        @pl.when(xs < n_xs - 1)
        def _():
            side(False)

    add_rows(0)

    def glow(q, sums):
        return tuple(
            sums[r]
            + gas[q, r] * out_ref(1)[q, row(r), :] * out_ref(0)[q, row(r), :]
            for r in range(ROWS)
        )

    zero = jnp.zeros((CHUNKS, LANES), jnp.float32)
    sums = lax.fori_loop(0, planes, glow, (zero,) * ROWS)
    for r in range(ROWS):
        img[pl.ds(r, CHUNKS, stride=CHUNKS), :] = sums[r]

    def img_copy(d):
        peer = lax.rem(ax + d, n_ax)
        tile = pl.ds(pl.multiple_of((peer // 2) * CHUNKS, CHUNKS), CHUNKS)
        return pltpu.make_async_remote_copy(
            src_ref=img.at[tile],
            dst_ref=img_in.at[d - 1],
            send_sem=img_send.at[d - 1],
            recv_sem=img_recv.at[d - 1],
            device_id=(peer, xs),
            device_id_type=MESH,
        )

    for d in range(1, n_ax):
        img_copy(d).start()

    add_rows(1)
    add_rows(2)

    mine = img[pl.ds(pl.multiple_of((ax // 2) * CHUNKS, CHUNKS), CHUNKS), :]
    for d in range(1, n_ax):
        img_copy(d).wait_recv()
        mine = mine + img_in[d - 1]
    half = LANES // 2
    mine = jnp.where(lax.rem(ax, 2) == 1, pltpu.roll(mine, half, 1), mine)
    image_out[...] = mine[:ROWS, :half] * (2.0 / total_planes) - picture_v[...]

    for d in range(1, n_ax):
        img_copy(d).wait_send()
    for part in range(4):
        @pl.when(ax > 0)
        def _():
            ax_copy(part, True).wait_send()

        @pl.when(ax < n_ax - 1)
        def _():
            ax_copy(part, False).wait_send()
    for group in range(3):
        for span in range(2):
            @pl.when(xs > 0)
            def _():
                xs_copy(group, span, True).wait_send()

            @pl.when(xs < n_xs - 1)
            def _():
                xs_copy(group, span, False).wait_send()


def tiled(x):
    *lead, rows, width = x.shape
    x = x.reshape(*lead, rows, width // LANES, LANES)
    return jnp.swapaxes(x, -3, -2).reshape(*lead, rows * (width // LANES), LANES)


def untiled(x, rows):
    *lead, both, lanes = x.shape
    x = x.reshape(*lead, both // rows, rows, lanes)
    return jnp.swapaxes(x, -3, -2).reshape(*lead, rows, (both // rows) * lanes)


def solution(mesh):
    n_ax, n_xs = mesh.shape["ax"], mesh.shape["xs"]

    def per_device(conc, temp, vel, gap, dest, rate_k, thresh, coeff, heat, picture):
        planes = conc.shape[1]
        total_planes = planes * n_ax
        f32 = jnp.float32
        any_space = pl.BlockSpec(memory_space=pltpu.HBM)
        vmem = pl.BlockSpec(memory_space=pltpu.VMEM)
        dma = pltpu.SemaphoreType.DMA
        both = ROWS * CHUNKS
        c, t, image = pl.pallas_call(
            functools.partial(per_device_kernel, n_ax, n_xs, planes, total_planes),
            out_shape=(
                jax.ShapeDtypeStruct((SPECIES, planes, both, LANES), f32),
                jax.ShapeDtypeStruct((planes, both, LANES), f32),
                jax.ShapeDtypeStruct(picture.shape, f32),
            ),
            in_specs=[any_space] * 10,
            out_specs=(vmem, vmem, vmem),
            scratch_shapes=[
                pltpu.VMEM((FIELDS, planes + 4, both, LANES), f32),
                pltpu.VMEM((FIELDS, planes + 2, ROWS + 2, CHUNKS, LANES), f32),
                pltpu.VMEM((3, planes, both, LANES), f32),
                pltpu.VMEM((planes, both, LANES), jnp.int32),
                pltpu.VMEM((6, ROWS, CHUNKS, LANES), f32),
                pltpu.VMEM((planes, 2, CHUNKS, LANES), f32),
                pltpu.VMEM((planes, ROWS, CHUNKS, LANES), f32),
                pltpu.SMEM((FIELDS * SPECIES,), f32),
                pltpu.VMEM((CHUNKS * CHUNKS, LANES), f32),
                pltpu.VMEM((n_ax - 1, CHUNKS, LANES), f32),
                dma((6,)),
                dma((6,)),
                dma((8,)),
                dma((8,)),
                dma((12,)),
                dma((12,)),
                dma((n_ax - 1,)),
                dma((n_ax - 1,)),
                pltpu.SMEM(dest.shape, jnp.int32),
                pltpu.SMEM(rate_k.shape, f32),
                pltpu.SMEM(thresh.shape, f32),
                pltpu.SMEM(coeff.shape, f32),
                pltpu.SMEM(heat.shape, f32),
                pltpu.VMEM(picture.shape, f32),
            ],
            compiler_params=pltpu.CompilerParams(
                collective_id=0, has_side_effects=True, vmem_limit_bytes=24 * 1024 * 1024
            ),
            name="fused_step",
        )(
            *(
                pltpu.with_memory_space_constraint(x, pltpu.HBM)
                for x in (
                    tiled(conc), tiled(temp), tiled(vel), tiled(gap),
                    dest, rate_k, thresh, coeff, heat, picture,
                )
            )
        )
        return untiled(c, ROWS), untiled(t, ROWS), image

    in_specs = (
        P(None, "ax", "xs", None),
        P("ax", "xs", None),
        P(None, "ax", "xs", None),
        P("ax", "xs", None),
        P(),
        P(),
        P(),
        P(),
        P(),
        P("xs", "ax"),
    )
    out_specs = (P(None, "ax", "xs", None), P("ax", "xs", None), P("xs", "ax"))
    return jax.shard_map(
        per_device, mesh=mesh, in_specs=in_specs, out_specs=out_specs, check_vma=False
    )
```

time: 95.7 us -> 39.3 us (0.41)
  Pallas kernels: 0 us -> 36 us
  local copies, waits for them, and re-layouts: 35.9 us -> 2.46 us
  starting transfers between devices: 25.5 us -> 0 us
  matrix products: 15.4 us -> 0 us
  other arithmetic: 10.5 us -> 0 us
  waiting for transfers between devices: 6.73 us -> 0 us
    pallas_call x0 -> x1, Pallas kernels: none -> 36 us  [per_device(): pl.pallas_call(functools.partial(per_device_kernel, n_ax, n_xs, planes, t...]
    ppermute x4 -> x0, starting transfers between devices: 17.5 us -> none  [the longest x1 9.37 us: with_halo(): lax.ppermute(lax.slice_in_dim(block, 0, width, axis=dim), axis, backward)]
    dot_general x3 -> x0, matrix products: 15.4 us -> none  [the longest x1 7.67 us: chemistry(): jnp.einsum('sr,ryz->syz', reaction_coefficient_matrix, flat, precision=la...]
    all_to_all x1 -> x0, starting transfers between devices: 8.02 us -> none  [sum_at_owner(): parts = lax.all_to_all(split_up(x, dim, count), axis, 0, 0, tiled=True)]
    slice x7 -> x0, local copies, waits for them, and re-layouts: 8.01 us -> none  [the longest x1 3.22 us: per_device(): upper_z = jnp.concatenate([remapped[..., 1:], zero_column], axis=3)]
    reshape x2 -> x0, local copies, waits for them, and re-layouts: 6.95 us -> none  [the longest x1 3.49 us: chemistry(): source = jnp.einsum('sr,ryz->syz', reaction_coefficient_matrix, flat, pre...]
    mul x5 -> x0, local copies, waits for them, and re-layouts: 5.48 us -> none  [the longest x2 2.88 us: per_device(): flow_speed_vector[0][None] * (upper_a - lower_a)]
    unnamed x28 -> x3, local copies, waits for them, and re-layouts: 7.61 us -> 2.46 us
  transfers between devices with their start and end apart: 5 -> 0, of which waited for: 2 -> 0; matrix products, arithmetic and copies ran while one was open for 41% -> 0% of each run, Pallas kernels for 0% -> 0%
where the time goes in v1:
time: 39.3 us; the launch traced here: 39.1 us
  Pallas kernels  36 us (92%)
  local copies, waits for them, and re-layouts  2.46 us (6%)
  between operations  0.64 us (2%)
    pallas_call x1, Pallas kernels, per_device(): pl.pallas_call(functools.partial(per_device_kernel, n_ax, n_xs, planes, t...  36 us
    unnamed x3, local copies, waits for them, and re-layouts  2.46 us

profile of v1, /device:TPU:9, one launch (start us, length us, event | category | flops | bytes accessed | tf_op | source)
XLA Modules:
  0.0 39.1 jit_solution(14641269265946284298)
XLA Ops:
  0.6 36.0 %fused_step.1 = (f32[9,12,32,128]{3,2,1,0:T(8,128)S(1)}, f32[12,32,128]{2,1,0:T(8,128)S(1)}, f32[4,64]{1,0:T(4,128)S(1)}) custom-call(f32[9,12,32,128]{3,2,1,0:T(8,128)} %bitcast.32, f32[12,32,128]{2,1,0:T(8,128)} %bitcast.34, f32[3,12,32,128]{3,2,1,0:T(8,128)} %bitcast.33, s32[12,32,128]{2,1,0:T(8,128)} %bitcast.35, s32[192]{0:T(256)} %dest.1, f32[9]{0:T(128)} %rate_k.1, ...), custom_call_target="tpu_custom_call" | custom-call | tf_op jit(solution)/shard_map/fused_step/pallas_call | solution.py:398
  36.7 1.2 %copy.22 = f32[9,12,4,1024]{3,2,1,0:T(4,128)} copy(f32[9,12,4,1024]{3,2,1,0:T(4,128)S(1)} %bitcast.30) | data formatting | bytes 3538944
  37.9 0.7 %copy.23 = f32[12,4,1024]{2,1,0:T(4,128)} copy(f32[12,4,1024]{2,1,0:T(4,128)S(1)} %bitcast.31) | data formatting | bytes 393216
  38.5 0.6 %copy.24 = f32[4,64]{1,0:T(4,128)} copy(f32[4,64]{1,0:T(4,128)S(1)} %get-tuple-element.14) | data formatting | bytes 2048

commit v2 on v1

--- a/solution.py
+++ b/solution.py
@@ -24,21 +24,30 @@
     conc_out, temp_out, image_out,
     old, rem, vel_v, gap_v, coef, edge, gas, mix, img, img_in,
     load_sem, small_sem, ax_send, ax_recv, xs_send, xs_recv, img_send, img_recv,
-    dest_s, rate_s, thresh_s, coeff_s, heat_s, picture_v,
+    known, dest_s, rate_s, thresh_s, coeff_s, heat_s, picture_v,
 ):
     ax = lax.axis_index("ax")
     xs = lax.axis_index("xs")
     start = ax * planes
 
     barrier = pltpu.get_barrier_semaphore()
-    for d in range(1, n_ax):
-        pl.semaphore_signal(
-            barrier, inc=1, device_id=(lax.rem(ax + d, n_ax), xs), device_id_type=MESH
-        )
-    for d in (1, n_xs - 1):
-        pl.semaphore_signal(
-            barrier, inc=1, device_id=(ax, lax.rem(xs + d, n_xs)), device_id_type=MESH
-        )
+    def greet(semaphore, distance):
+        for d in (distance, n_ax - distance):
+            pl.semaphore_signal(
+                semaphore, inc=1, device_id=(lax.rem(ax + d, n_ax), xs), device_id_type=MESH
+            )
+
+    greet(barrier, 1)
+    has_low, has_high = xs > 0, xs < n_xs - 1
+
+    @pl.when(has_low)
+    def _():
+        pl.semaphore_signal(barrier, inc=1, device_id=(ax, xs - 1), device_id_type=MESH)
+
+    @pl.when(has_high)
+    def _():
+        pl.semaphore_signal(barrier, inc=1, device_id=(ax, xs + 1), device_id_type=MESH)
+
 
     def local(src, dst, sem):
         copy = pltpu.make_async_copy(src, dst, sem)
@@ -122,24 +131,47 @@
     down = (lax.max(ax - 1, 0), xs)
     up = (lax.min(ax + 1, n_ax - 1), xs)
     low3, top3 = pl.ds(0, 3), pl.ds(planes + 1, 3)
-    ax_parts = (
-        (lambda s: temp.at[s], (0,)),
-        (lambda s: conc.at[4, s], (1,)),
-        (lambda s: conc.at[pl.ds(0, 4), s], (pl.ds(2, 4),)),
-        (lambda s: conc.at[pl.ds(5, 4), s], (pl.ds(6, 4),)),
+    low2, top2 = pl.ds(0, 2), pl.ds(planes + 1, 2)
+    firsts, lasts = pl.ds(0, 4), pl.ds(2, 4)
+    seconds, ends = pl.ds(5, 4), pl.ds(6, 4)
+    down_parts = (
+        (temp.at[low3], (0, top3)),
+        (conc.at[4, low3], (1, top3)),
+        (conc.at[firsts, low2], (lasts, top2)),
+        (conc.at[seconds, low2], (ends, top2)),
+        (conc.at[firsts, 2], (lasts, planes + 3)),
+        (conc.at[seconds, 2], (ends, planes + 3)),
     )
+    up_parts = (
+        (temp.at[planes - 1], (0, 0)),
+        (conc.at[4, planes - 1], (1, 0)),
+        (conc.at[firsts, planes - 1], (lasts, 0)),
+        (conc.at[seconds, planes - 1], (ends, 0)),
+    )
 
     def ax_copy(part, going_down):
-        source, where = ax_parts[part]
-        slot = 2 * part + (0 if going_down else 1)
+        source, where = (down_parts if going_down else up_parts)[part]
+        slot = part + (0 if going_down else len(down_parts))
         return pltpu.make_async_remote_copy(
-            src_ref=source(low3 if going_down else planes - 1),
-            dst_ref=old.at[where + ((top3 if going_down else 0),)],
+            src_ref=source,
+            dst_ref=old.at[where],
             send_sem=ax_send.at[slot],
             recv_sem=ax_recv.at[slot],
             device_id=down if going_down else up,
             device_id_type=MESH,
         )
+
+    def each_down(parts, sending, act):
+        @pl.when(ax > 0 if sending else ax < n_ax - 1)
+        def _():
+            for part in parts:
+                act(ax_copy(part, True))
+
+    def each_up(parts, sending, act):
+        @pl.when(ax < n_ax - 1 if sending else ax > 0)
+        def _():
+            for part in parts:
+                act(ax_copy(part, False))
 
     spans = (pl.ds(1, planes - 2), pl.ds(planes - 1, 2))
 
@@ -169,24 +201,18 @@
     loads[0].wait()
     loads[1].wait()
     remap(0, 2, 0, planes - 2)
-    pl.semaphore_wait(barrier, n_ax + 1)
-
-    for part in range(4):
-        @pl.when(ax > 0)
-        def _():
-            ax_copy(part, True).start()
-
-        @pl.when(ax < n_ax - 1)
-        def _():
-            ax_copy(part, False).start()
-
-    xs_start(0, 0)
     loads[2].wait()
     remap(2, 4, 0, planes - 2)
-    xs_start(1, 0)
     loads[3].wait()
     remap(6, 4, 0, planes - 2)
-    xs_start(2, 0)
+    pl.semaphore_wait(barrier, 2 + has_low.astype(jnp.int32) + has_high.astype(jnp.int32))
+
+    each_down(range(2), True, lambda c: c.start())
+    xs_start(0, 0)
+    each_down(range(2, 6), True, lambda c: c.start())
+    each_up(range(4), True, lambda c: c.start())
+    xs_start(1, 0)
+    greet(known.at[0], 1)
     for small in smalls[1:]:
         small.wait()
     loads[4].wait()
@@ -266,24 +292,27 @@
 
         lax.fori_loop(0, count, body, 0)
 
-    run_planes(1, planes - 4)
-
-    for group, parts in enumerate(((0, 1), (2,), (3,))):
-        for part in parts:
-            @pl.when(ax < n_ax - 1)
-            def _():
-                ax_copy(part, True).wait_recv()
-
-            @pl.when(ax > 0)
-            def _():
-                ax_copy(part, False).wait_recv()
-        f0, fn = GROUPS[group]
-        remap(f0, fn, planes - 2, 3)
-        xs_start(group, 1)
-        remap_low(f0, fn)
-
+    run_planes(1, 4)
+    each_down(range(2), False, lambda c: c.wait_recv())
+    remap(0, 2, planes - 2, 3)
+    xs_start(0, 1)
+    xs_start(2, 0)
+    pl.semaphore_wait(known.at[0], 2)
+    greet(known.at[1], 2)
+    run_planes(5, planes - 8)
+    each_down(range(2, 4), False, lambda c: c.wait_recv())
+    remap(2, 8, planes - 2, 2)
+    xs_start(1, 1)
+    xs_start(2, 1)
+    pl.semaphore_wait(known.at[1], 2)
+    greet(known.at[2], 4)
+    each_up(range(4), False, lambda c: c.wait_recv())
+    remap_low(0, FIELDS)
     run_planes(0, 1)
-    run_planes(planes - 3, 3)
+    run_planes(planes - 3, 1)
+    each_down(range(4, 6), False, lambda c: c.wait_recv())
+    remap(2, 8, planes, 1)
+    run_planes(planes - 2, 2)
 
     def add_rows(group):
         f0, fn = GROUPS[group]
@@ -337,6 +366,7 @@
             device_id_type=MESH,
         )
 
+    pl.semaphore_wait(known.at[2], 2)
     for d in range(1, n_ax):
         img_copy(d).start()
 
@@ -353,14 +383,8 @@
 
     for d in range(1, n_ax):
         img_copy(d).wait_send()
-    for part in range(4):
-        @pl.when(ax > 0)
-        def _():
-            ax_copy(part, True).wait_send()
-
-        @pl.when(ax < n_ax - 1)
-        def _():
-            ax_copy(part, False).wait_send()
+    each_down(range(6), True, lambda c: c.wait_send())
+    each_up(range(4), True, lambda c: c.wait_send())
     for group in range(3):
         for span in range(2):
             @pl.when(xs > 0)
@@ -417,12 +441,13 @@
                 pltpu.VMEM((n_ax - 1, CHUNKS, LANES), f32),
                 dma((6,)),
                 dma((6,)),
-                dma((8,)),
-                dma((8,)),
+                dma((10,)),
+                dma((10,)),
                 dma((12,)),
                 dma((12,)),
                 dma((n_ax - 1,)),
                 dma((n_ax - 1,)),
+                pltpu.SemaphoreType.REGULAR((3,)),
                 pltpu.SMEM(dest.shape, jnp.int32),
                 pltpu.SMEM(rate_k.shape, f32),
                 pltpu.SMEM(thresh.shape, f32),

time: 39.3 us -> 31.9 us (0.81)
  the two profiles are of different devices: /device:TPU:9 before, /device:TPU:1 now
where the time goes in v2:
time: 31.9 us; the launch traced here: 31.7 us
  Pallas kernels  28.6 us (90%)
  local copies, waits for them, and re-layouts  2.46 us (8%)
  between operations  0.64 us (2%)
    pallas_call x1, Pallas kernels, per_device(): pl.pallas_call(functools.partial(per_device_kernel, n_ax, n_xs, planes, t...  28.6 us
    unnamed x3, local copies, waits for them, and re-layouts  2.46 us

profile of v2, /device:TPU:1, one launch (start us, length us, event | category | flops | bytes accessed | tf_op | source)
XLA Modules:
  0.0 31.7 jit_solution(8699397563926259724)
XLA Ops:
  0.6 28.6 %fused_step.1 = (f32[9,12,32,128]{3,2,1,0:T(8,128)S(1)}, f32[12,32,128]{2,1,0:T(8,128)S(1)}, f32[4,64]{1,0:T(4,128)S(1)}) custom-call(f32[9,12,32,128]{3,2,1,0:T(8,128)} %bitcast.32, f32[12,32,128]{2,1,0:T(8,128)} %bitcast.34, f32[3,12,32,128]{3,2,1,0:T(8,128)} %bitcast.33, s32[12,32,128]{2,1,0:T(8,128)} %bitcast.35, s32[192]{0:T(256)} %dest.1, f32[9]{0:T(128)} %rate_k.1, ...), custom_call_target="tpu_custom_call" | custom-call | tf_op jit(solution)/shard_map/fused_step/pallas_call | solution.py:422
  29.2 1.2 %copy.22 = f32[9,12,4,1024]{3,2,1,0:T(4,128)} copy(f32[9,12,4,1024]{3,2,1,0:T(4,128)S(1)} %bitcast.30) | data formatting | bytes 3538944
  30.5 0.7 %copy.23 = f32[12,4,1024]{2,1,0:T(4,128)} copy(f32[12,4,1024]{2,1,0:T(4,128)S(1)} %bitcast.31) | data formatting | bytes 393216
  31.1 0.6 %copy.24 = f32[4,64]{1,0:T(4,128)} copy(f32[4,64]{1,0:T(4,128)S(1)} %get-tuple-element.14) | data formatting | bytes 2048

commit v3 on v2

--- a/solution.py
+++ b/solution.py
@@ -11,7 +11,8 @@
 FIELDS = 10
 ORDER = (9, 4, 0, 1, 2, 3, 5, 6, 7, 8)
 PLACE = tuple(ORDER.index(f) for f in range(FIELDS))
-GROUPS = ((0, 2), (2, 4), (6, 4))
+GROUPS = ((0, 2), (2, 2), (4, 2), (6, 2), (8, 2))
+RELAYED = (3, 4)
 ROWS = 4
 LANES = 128
 CHUNKS = 8
@@ -22,8 +23,8 @@
     n_ax, n_xs, planes, total_planes,
     conc, temp, vel, gap, dest, rate_k, thresh, coeff, heat, picture,
     conc_out, temp_out, image_out,
-    old, rem, vel_v, gap_v, coef, edge, gas, mix, img, img_in,
-    load_sem, small_sem, ax_send, ax_recv, xs_send, xs_recv, img_send, img_recv,
+    old, rem, relay, pack, tail, vel_v, gap_v, coef, edge, gas, mix, img, img_in,
+    load_sem, small_sem, ax_send, ax_recv, xs_send, xs_recv, relay_send, relay_recv, tail_send, tail_recv, img_send, img_recv,
     known, dest_s, rate_s, thresh_s, coeff_s, heat_s, picture_v,
 ):
     ax = lax.axis_index("ax")
@@ -32,22 +33,53 @@
 
     barrier = pltpu.get_barrier_semaphore()
     def greet(semaphore, distance):
-        for d in (distance, n_ax - distance):
+        @pl.when(ax >= distance)
+        def _():
             pl.semaphore_signal(
-                semaphore, inc=1, device_id=(lax.rem(ax + d, n_ax), xs), device_id_type=MESH
+                semaphore, inc=1, device_id=(ax - distance, xs), device_id_type=MESH
             )
+
+        @pl.when(ax < n_ax - distance)
+        def _():
+            pl.semaphore_signal(
+                semaphore, inc=1, device_id=(ax + distance, xs), device_id_type=MESH
+            )
+
+    def greeters(distance):
+        return (ax >= distance).astype(jnp.int32) + (ax < n_ax - distance).astype(jnp.int32)
 
     greet(barrier, 1)
     has_low, has_high = xs > 0, xs < n_xs - 1
+    middle = n_xs // 2
+    below_middle, above_middle = xs == middle - 1, xs == middle
+
+    def signal_xs(semaphore, target):
+        pl.semaphore_signal(semaphore, inc=1, device_id=(ax, target), device_id_type=MESH)
 
     @pl.when(has_low)
     def _():
-        pl.semaphore_signal(barrier, inc=1, device_id=(ax, xs - 1), device_id_type=MESH)
-
-    @pl.when(has_high)
+        signal_xs(barrier, xs - 1)
+
+    @pl.when(has_high & ~below_middle)
     def _():
-        pl.semaphore_signal(barrier, inc=1, device_id=(ax, xs + 1), device_id_type=MESH)
-
+        signal_xs(barrier, xs + 1)
+
+    far_slab, after_far = ax == n_ax // 2 - 1, ax == n_ax // 2
+
+    @pl.when(above_middle & far_slab)
+    def _():
+        pl.semaphore_signal(
+            barrier, inc=1, device_id=(ax + 1, middle - 1), device_id_type=MESH
+        )
+
+    @pl.when(xs == 0)
+    def _():
+        signal_xs(barrier, middle)
+        signal_xs(barrier, middle - 1)
+
+    @pl.when(xs == n_xs - 1)
+    def _():
+        signal_xs(barrier, middle - 1)
 
     def local(src, dst, sem):
         copy = pltpu.make_async_copy(src, dst, sem)
@@ -188,30 +220,161 @@
             device_id_type=MESH,
         )
 
+    def to_relay(group, going_down):
+        f0, fn = GROUPS[group]
+        slot = group - RELAYED[0]
+        return pltpu.make_async_remote_copy(
+            src_ref=rem.at[pl.ds(f0, fn), spans[0], 1 if going_down else ROWS],
+            dst_ref=relay.at[pl.ds(2 * slot, fn)],
+            send_sem=xs_send.at[4 * group + (0 if going_down else 1)],
+            recv_sem=relay_recv.at[slot],
+            device_id=(ax, 0 if going_down else n_xs - 1),
+            device_id_type=MESH,
+        )
+
+    def from_relay(group, going_down):
+        f0, fn = GROUPS[group]
+        slot = group - RELAYED[0]
+        return pltpu.make_async_remote_copy(
+            src_ref=relay.at[pl.ds(2 * slot, fn)],
+            dst_ref=rem.at[pl.ds(f0, fn), spans[0], ROWS + 1 if going_down else 0],
+            send_sem=relay_send.at[slot],
+            recv_sem=xs_recv.at[4 * group + (0 if going_down else 1)],
+            device_id=(ax, middle - 1 if going_down else middle),
+            device_id_type=MESH,
+        )
+
+    def goes_round(group):
+        return (ax < n_ax - 2) | (group == RELAYED[-1])
+
+    tail_fields = (pl.ds(0, 2), pl.ds(2, FIELDS - 2))
+
+    def tail_copy(part, next_slab):
+        fields = tail_fields[part]
+        two = pl.ds(2 if next_slab else 0, 2)
+        slot = 2 * part + (1 if next_slab else 0)
+        return pltpu.make_async_remote_copy(
+            src_ref=pack.at[fields, two],
+            dst_ref=tail.at[fields, two],
+            send_sem=tail_send.at[slot],
+            recv_sem=tail_recv.at[slot],
+            device_id=(lax.max(ax - 1, 0) if next_slab else ax, middle),
+            device_id_type=MESH,
+        )
+
+    def tail_start(part):
+        first, count = ((0, 2), (2, FIELDS - 2))[part]
+
+        def send(next_slab, sources):
+            for f in range(first, first + count):
+                for k, p in sources:
+                    pack[f, k] = old[f, p, row(ROWS - 1), :]
+            tail_copy(part, next_slab).start()
+
+        @pl.when(below_middle & far_slab)
+        def _():
+            send(False, ((0, planes - 1), (1, planes)))
+
+        @pl.when(below_middle & after_far)
+        def _():
+            send(True, ((2, 1), (3, 2)))
+
+    def tail_end():
+        for next_slab, here in ((False, far_slab), (True, after_far)):
+            @pl.when(below_middle & here)
+            def _():
+                for part in range(2):
+                    tail_copy(part, next_slab).wait_send()
+
+    def tail_rows(part):
+        first, count = ((0, 2), (2, FIELDS - 2))[part]
+
+        @pl.when(above_middle & far_slab)
+        def _():
+            tail_copy(part, True).wait_recv()
+            tail_copy(part, False).wait_recv()
+            for k in range(2):
+                w = weights(planes - 2 + k)
+                for f in range(first, first + count):
+                    rem[f, planes - 1 + k, 0] = (
+                        w[0] * tail[f, k] + w[1] * tail[f, k + 1] + w[2] * tail[f, k + 2]
+                    )
+
+    def middle_start(group):
+        @pl.when(below_middle & goes_round(group))
+        def _():
+            to_relay(group, False).start()
+
+        @pl.when(above_middle)
+        def _():
+            to_relay(group, True).start()
+
     def xs_start(group, span):
-        @pl.when(xs > 0)
+        @pl.when(has_low & ~above_middle)
         def _():
             xs_copy(group, span, True).start()
 
-        @pl.when(xs < n_xs - 1)
+        relayed = group in RELAYED and span == 0
+
+        elsewhere = goes_round(group) if relayed else far_slab
+
+        @pl.when(has_high & ~(below_middle & elsewhere) if relayed or span == 1 else has_high)
         def _():
             xs_copy(group, span, False).start()
+
+    def late_start():
+        @pl.when(above_middle)
+        def _():
+            pl.semaphore_wait(known.at[4], 1)
+            for group in range(5):
+                for span in range(2):
+                    if span == 1 or group not in RELAYED:
+                        xs_copy(group, span, True).start()
+
+    def pass_on(group, going_down):
+        @pl.when((xs == (0 if going_down else n_xs - 1)) & (going_down | goes_round(group)))
+        def _():
+            if going_down and group == RELAYED[0]:
+                pl.semaphore_wait(known.at[4], 1)
+            to_relay(group, going_down).wait_recv()
+            from_relay(group, going_down).start()
+
+    def pass_end(going_down):
+        for group in RELAYED:
+            @pl.when((xs == (0 if going_down else n_xs - 1)) & (going_down | goes_round(group)))
+            def _():
+                from_relay(group, going_down).wait_send()
+
+    greeted = greeters(1) + has_high.astype(jnp.int32) + (has_low & ~above_middle).astype(jnp.int32)
+    pl.semaphore_wait(
+        barrier,
+        greeted
+        + 2 * below_middle.astype(jnp.int32)
+        + above_middle.astype(jnp.int32)
+        + (below_middle & after_far).astype(jnp.int32),
+    )
+    each_down(range(6), True, lambda c: c.start())
+    each_up(range(4), True, lambda c: c.start())
+
+    @pl.when(below_middle)
+    def _():
+        signal_xs(known.at[4], middle)
+        signal_xs(known.at[4], 0)
 
     smalls[0].wait()
     loads[0].wait()
     loads[1].wait()
     remap(0, 2, 0, planes - 2)
+    xs_start(0, 0)
+    tail_start(0)
     loads[2].wait()
     remap(2, 4, 0, planes - 2)
+    xs_start(1, 0)
     loads[3].wait()
     remap(6, 4, 0, planes - 2)
-    pl.semaphore_wait(barrier, 2 + has_low.astype(jnp.int32) + has_high.astype(jnp.int32))
-
-    each_down(range(2), True, lambda c: c.start())
-    xs_start(0, 0)
-    each_down(range(2, 6), True, lambda c: c.start())
-    each_up(range(4), True, lambda c: c.start())
-    xs_start(1, 0)
+    middle_start(3)
+    middle_start(4)
+    tail_start(1)
     greet(known.at[0], 1)
     for small in smalls[1:]:
         small.wait()
@@ -235,7 +398,7 @@
         f = ORDER[i]
         return temp_out if f == SPECIES else conc_out.at[f]
 
-    def plane(q):
+    def plane(q, fields=range(FIELDS)):
         for r in range(ROWS):
             for d in range(3):
                 v = 0.1 * vel_v[d, q, row(r), :]
@@ -261,7 +424,7 @@
                     for s in range(SPECIES)
                 ]
             )
-        for i in range(FIELDS):
+        for i in fields:
             f = ORDER[i]
             source = [None] * ROWS
             for s in range(SPECIES):
@@ -296,23 +459,27 @@
     each_down(range(2), False, lambda c: c.wait_recv())
     remap(0, 2, planes - 2, 3)
     xs_start(0, 1)
-    xs_start(2, 0)
-    pl.semaphore_wait(known.at[0], 2)
+    for group in range(2, 5):
+        xs_start(group, 0)
+    pl.semaphore_wait(known.at[0], greeters(1))
     greet(known.at[1], 2)
+    pass_on(3, False)
     run_planes(5, planes - 8)
+    pl.semaphore_wait(known.at[1], greeters(2))
+    greet(known.at[2], 4)
+    pass_on(4, False)
     each_down(range(2, 4), False, lambda c: c.wait_recv())
     remap(2, 8, planes - 2, 2)
-    xs_start(1, 1)
-    xs_start(2, 1)
-    pl.semaphore_wait(known.at[1], 2)
-    greet(known.at[2], 4)
+    for group in range(1, 5):
+        xs_start(group, 1)
+    pl.semaphore_wait(known.at[2], greeters(4))
+    greet(known.at[3], 8)
     each_up(range(4), False, lambda c: c.wait_recv())
     remap_low(0, FIELDS)
     run_planes(0, 1)
-    run_planes(planes - 3, 1)
-    each_down(range(4, 6), False, lambda c: c.wait_recv())
-    remap(2, 8, planes, 1)
-    run_planes(planes - 2, 2)
+    run_planes(planes - 3, 2)
+    plane(planes - 1, range(2))
+    late_start()
 
     def add_rows(group):
         f0, fn = GROUPS[group]
@@ -328,8 +495,13 @@
                     ref[q, row(r), :] = ref[q, row(r), :] + c * rem[i, q + 1, halo]
                 return carry
 
-            for span in range(2):
-                xs_copy(group, span, not is_low).wait_recv()
+            xs_copy(group, 0, not is_low).wait_recv()
+            if is_low:
+                @pl.when(~(above_middle & far_slab))
+                def _():
+                    xs_copy(group, 1, False).wait_recv()
+            else:
+                xs_copy(group, 1, True).wait_recv()
             lax.fori_loop(0, planes, body, 0)
 
         @pl.when(xs > 0)
@@ -340,6 +512,7 @@
         def _():
             side(False)
 
+    tail_rows(0)
     add_rows(0)
 
     def glow(q, sums):
@@ -366,12 +539,18 @@
             device_id_type=MESH,
         )
 
-    pl.semaphore_wait(known.at[2], 2)
+    pl.semaphore_wait(known.at[3], greeters(8))
     for d in range(1, n_ax):
         img_copy(d).start()
 
-    add_rows(1)
-    add_rows(2)
+    each_down(range(4, 6), False, lambda c: c.wait_recv())
+    remap(2, 8, planes, 1)
+    plane(planes - 1, range(2, FIELDS))
+    tail_rows(1)
+    for group in RELAYED:
+        pass_on(group, True)
+    for group in range(1, 5):
+        add_rows(group)
 
     mine = img[pl.ds(pl.multiple_of((ax // 2) * CHUNKS, CHUNKS), CHUNKS), :]
     for d in range(1, n_ax):
@@ -385,15 +564,31 @@
         img_copy(d).wait_send()
     each_down(range(6), True, lambda c: c.wait_send())
     each_up(range(4), True, lambda c: c.wait_send())
-    for group in range(3):
+    tail_end()
+    pass_end(False)
+    pass_end(True)
+    for group in range(5):
         for span in range(2):
-            @pl.when(xs > 0)
+            @pl.when(has_low)
             def _():
                 xs_copy(group, span, True).wait_send()
 
-            @pl.when(xs < n_xs - 1)
+            @pl.when(has_high & ~(below_middle & far_slab) if span == 1 else has_high)
             def _():
                 xs_copy(group, span, False).wait_send()
+
+
+def write_out(c, t, image, c_out, t_out, image_out, sem):
+    copies = [
+        pltpu.make_async_copy(c.at[pl.ds(3 * i, 3)], c_out.at[pl.ds(3 * i, 3)], sem.at[i])
+        for i in range(3)
+    ]
+    copies.append(pltpu.make_async_copy(t, t_out, sem.at[3]))
+    copies.append(pltpu.make_async_copy(image, image_out, sem.at[4]))
+    for copy in copies:
+        copy.start()
+    for copy in copies:
+        copy.wait()
 
 
 def tiled(x):
@@ -431,6 +626,9 @@
             scratch_shapes=[
                 pltpu.VMEM((FIELDS, planes + 4, both, LANES), f32),
                 pltpu.VMEM((FIELDS, planes + 2, ROWS + 2, CHUNKS, LANES), f32),
+                pltpu.VMEM((4, planes - 2, CHUNKS, LANES), f32),
+                pltpu.VMEM((FIELDS, 4, CHUNKS, LANES), f32),
+                pltpu.VMEM((FIELDS, 4, CHUNKS, LANES), f32),
                 pltpu.VMEM((3, planes, both, LANES), f32),
                 pltpu.VMEM((planes, both, LANES), jnp.int32),
                 pltpu.VMEM((6, ROWS, CHUNKS, LANES), f32),
@@ -443,11 +641,15 @@
                 dma((6,)),
                 dma((10,)),
                 dma((10,)),
-                dma((12,)),
-                dma((12,)),
+                dma((20,)),
+                dma((20,)),
+                dma((2,)),
+                dma((2,)),
+                dma((4,)),
+                dma((4,)),
                 dma((n_ax - 1,)),
                 dma((n_ax - 1,)),
-                pltpu.SemaphoreType.REGULAR((3,)),
+                pltpu.SemaphoreType.REGULAR((5,)),
                 pltpu.SMEM(dest.shape, jnp.int32),
                 pltpu.SMEM(rate_k.shape, f32),
                 pltpu.SMEM(thresh.shape, f32),
@@ -468,6 +670,16 @@
                 )
             )
         )
+        either = pl.BlockSpec(memory_space=pl.ANY)
+        c, t, image = pl.pallas_call(
+            write_out,
+            out_shape=tuple(jax.ShapeDtypeStruct(x.shape, f32) for x in (c, t, image)),
+            in_specs=[either] * 3,
+            out_specs=(either,) * 3,
+            scratch_shapes=[dma((5,))],
+            compiler_params=pltpu.CompilerParams(vmem_limit_bytes=4 * 1024 * 1024),
+            name="write_out",
+        )(*(pltpu.with_memory_space_constraint(x, pltpu.VMEM) for x in (c, t, image)))
         return untiled(c, ROWS), untiled(t, ROWS), image
 
     in_specs = (

time: 31.9 us -> 28.1 us (0.88)
  the two profiles are of different devices: /device:TPU:1 before, /device:TPU:9 now
where the time goes in v3:
time: 28.1 us; the launch traced here: 27.9 us
  Pallas kernels  27.3 us (97%)
  between operations  0.64 us (2%)
    pallas_call x1, Pallas kernels, per_device(): pl.pallas_call(functools.partial(per_device_kernel, n_ax, n_xs, planes, t...  26 us
    pallas_call x1, Pallas kernels, per_device(): pl.pallas_call(write_out, out_shape=tuple((jax.ShapeDtypeStruct(x.shape,...  1.31 us

profile of v3, /device:TPU:9, one launch (start us, length us, event | category | flops | bytes accessed | tf_op | source)
XLA Modules:
  0.0 27.9 jit_solution(14940385182703914448)
XLA Ops:
  0.6 26.0 %fused_step.1 = (f32[9,12,32,128]{3,2,1,0:T(8,128)S(1)}, f32[12,32,128]{2,1,0:T(8,128)S(1)}, f32[4,64]{1,0:T(4,128)S(1)}) custom-call(f32[9,12,32,128]{3,2,1,0:T(8,128)} %bitcast.30, f32[12,32,128]{2,1,0:T(8,128)} %bitcast.32, f32[3,12,32,128]{3,2,1,0:T(8,128)} %bitcast.31, s32[12,32,128]{2,1,0:T(8,128)} %bitcast.33, s32[192]{0:T(256)} %dest.1, f32[9]{0:T(128)} %rate_k.1, ...), custom_call_target="tpu_custom_call" | custom-call | tf_op jit(solution)/shard_map/fused_step/pallas_call | solution.py:617
  26.6 1.3 %write_out.1 = (f32[9,12,32,128]{3,2,1,0:T(8,128)}, f32[12,32,128]{2,1,0:T(8,128)}, f32[4,64]{1,0:T(4,128)}) custom-call(f32[9,12,32,128]{3,2,1,0:T(8,128)S(1)} %get-tuple-element.9.c, f32[12,32,128]{2,1,0:T(8,128)S(1)} %get-tuple-element.10.t, f32[4,64]{1,0:T(4,128)S(1)} %get-tuple-element.11.image), custom_call_target="tpu_custom_call" | custom-call | tf_op jit(solution)/shard_map/write_out/pallas_call | solution.py:674

commit v4 on v3

--- a/solution.py
+++ b/solution.py
@@ -345,6 +345,10 @@
             def _():
                 from_relay(group, going_down).wait_send()
 
+    smalls[0].wait()
+    loads[0].wait()
+    loads[1].wait()
+    remap(0, 2, 0, planes - 2)
     greeted = greeters(1) + has_high.astype(jnp.int32) + (has_low & ~above_middle).astype(jnp.int32)
     pl.semaphore_wait(
         barrier,
@@ -353,20 +357,16 @@
         + above_middle.astype(jnp.int32)
         + (below_middle & after_far).astype(jnp.int32),
     )
-    each_down(range(6), True, lambda c: c.start())
-    each_up(range(4), True, lambda c: c.start())
+    xs_start(0, 0)
+    each_down(range(2), True, lambda c: c.start())
+    tail_start(0)
+    each_down(range(2, 6), True, lambda c: c.start())
 
     @pl.when(below_middle)
     def _():
         signal_xs(known.at[4], middle)
         signal_xs(known.at[4], 0)
 
-    smalls[0].wait()
-    loads[0].wait()
-    loads[1].wait()
-    remap(0, 2, 0, planes - 2)
-    xs_start(0, 0)
-    tail_start(0)
     loads[2].wait()
     remap(2, 4, 0, planes - 2)
     xs_start(1, 0)
@@ -375,6 +375,7 @@
     middle_start(3)
     middle_start(4)
     tail_start(1)
+    each_up(range(4), True, lambda c: c.start())
     greet(known.at[0], 1)
     for small in smalls[1:]:
         small.wait()
@@ -540,7 +541,7 @@
         )
 
     pl.semaphore_wait(known.at[3], greeters(8))
-    for d in range(1, n_ax):
+    for d in sorted(range(1, n_ax), key=lambda d: abs(d - n_ax // 2)):
         img_copy(d).start()
 
     each_down(range(4, 6), False, lambda c: c.wait_recv())

time: 28.1 us -> 27.9 us (level)
  the two profiles are of different devices: /device:TPU:9 before, /device:TPU:7 now
where the time goes in v4:
time: 27.9 us; the launch traced here: 27.8 us
  Pallas kernels  27.2 us (97%)
  between operations  0.64 us (2%)
    pallas_call x1, Pallas kernels, per_device(): pl.pallas_call(functools.partial(per_device_kernel, n_ax, n_xs, planes, t...  25.9 us
    pallas_call x1, Pallas kernels, per_device(): pl.pallas_call(write_out, out_shape=tuple((jax.ShapeDtypeStruct(x.shape,...  1.31 us

profile of v4, /device:TPU:7, one launch (start us, length us, event | category | flops | bytes accessed | tf_op | source)
XLA Modules:
  0.0 27.8 jit_solution(17724266925804278985)
XLA Ops:
  0.6 25.9 %fused_step.1 = (f32[9,12,32,128]{3,2,1,0:T(8,128)S(1)}, f32[12,32,128]{2,1,0:T(8,128)S(1)}, f32[4,64]{1,0:T(4,128)S(1)}) custom-call(f32[9,12,32,128]{3,2,1,0:T(8,128)} %bitcast.30, f32[12,32,128]{2,1,0:T(8,128)} %bitcast.32, f32[3,12,32,128]{3,2,1,0:T(8,128)} %bitcast.31, s32[12,32,128]{2,1,0:T(8,128)} %bitcast.33, s32[192]{0:T(256)} %dest.1, f32[9]{0:T(128)} %rate_k.1, ...), custom_call_target="tpu_custom_call" | custom-call | tf_op jit(solution)/shard_map/fused_step/pallas_call | solution.py:618
  26.5 1.3 %write_out.1 = (f32[9,12,32,128]{3,2,1,0:T(8,128)}, f32[12,32,128]{2,1,0:T(8,128)}, f32[4,64]{1,0:T(4,128)}) custom-call(f32[9,12,32,128]{3,2,1,0:T(8,128)S(1)} %get-tuple-element.9.c, f32[12,32,128]{2,1,0:T(8,128)S(1)} %get-tuple-element.10.t, f32[4,64]{1,0:T(4,128)S(1)} %get-tuple-element.11.image), custom_call_target="tpu_custom_call" | custom-call | tf_op jit(solution)/shard_map/write_out/pallas_call | solution.py:675

commit v5 on v4

--- a/solution.py
+++ b/solution.py
@@ -456,7 +456,7 @@
 
         lax.fori_loop(0, count, body, 0)
 
-    run_planes(1, 4)
+    run_planes(1, 2)
     each_down(range(2), False, lambda c: c.wait_recv())
     remap(0, 2, planes - 2, 3)
     xs_start(0, 1)
@@ -465,7 +465,7 @@
     pl.semaphore_wait(known.at[0], greeters(1))
     greet(known.at[1], 2)
     pass_on(3, False)
-    run_planes(5, planes - 8)
+    run_planes(3, planes - 6)
     pl.semaphore_wait(known.at[1], greeters(2))
     greet(known.at[2], 4)
     pass_on(4, False)

time: 27.9 us -> 28 us (level)
  no operation moved by 1% of the time
where the time goes in v5:
time: 28 us; the launch traced here: 27.8 us
  Pallas kernels  27.2 us (97%)
  between operations  0.64 us (2%)
    pallas_call x1, Pallas kernels, per_device(): pl.pallas_call(functools.partial(per_device_kernel, n_ax, n_xs, planes, t...  25.9 us
    pallas_call x1, Pallas kernels, per_device(): pl.pallas_call(write_out, out_shape=tuple((jax.ShapeDtypeStruct(x.shape,...  1.31 us

profile of v5, /device:TPU:7, one launch (start us, length us, event | category | flops | bytes accessed | tf_op | source)
XLA Modules:
  0.0 27.8 jit_solution(3072724236826928571)
XLA Ops:
  0.6 25.9 %fused_step.1 = (f32[9,12,32,128]{3,2,1,0:T(8,128)S(1)}, f32[12,32,128]{2,1,0:T(8,128)S(1)}, f32[4,64]{1,0:T(4,128)S(1)}) custom-call(f32[9,12,32,128]{3,2,1,0:T(8,128)} %bitcast.30, f32[12,32,128]{2,1,0:T(8,128)} %bitcast.32, f32[3,12,32,128]{3,2,1,0:T(8,128)} %bitcast.31, s32[12,32,128]{2,1,0:T(8,128)} %bitcast.33, s32[192]{0:T(256)} %dest.1, f32[9]{0:T(128)} %rate_k.1, ...), custom_call_target="tpu_custom_call" | custom-call | tf_op jit(solution)/shard_map/fused_step/pallas_call | solution.py:618
  26.5 1.3 %write_out.1 = (f32[9,12,32,128]{3,2,1,0:T(8,128)}, f32[12,32,128]{2,1,0:T(8,128)}, f32[4,64]{1,0:T(4,128)}) custom-call(f32[9,12,32,128]{3,2,1,0:T(8,128)S(1)} %get-tuple-element.9.c, f32[12,32,128]{2,1,0:T(8,128)S(1)} %get-tuple-element.10.t, f32[4,64]{1,0:T(4,128)S(1)} %get-tuple-element.11.image), custom_call_target="tpu_custom_call" | custom-call | tf_op jit(solution)/shard_map/write_out/pallas_call | solution.py:675
